TPU v7x, 32 devices: a whole 2x2x4 slice. The times are simulated.
32 devices in a mesh: seq: 16 (over z, y, core), tensor: 2 (over x).
Axes of the slice: x: 2, y: 2, z: 4, core: 2. Of those that a mesh axis runs over, the one named last changes fastest.
Arguments:
- queries: bfloat16 [4096, 3072], P('seq', 'tensor'), may hold values from -100 to 100
- key_tiles: bfloat16 [4096, 3072], P('seq', 'tensor'), may hold values from -6 to 6
- value_tiles: bfloat16 [4096, 3072], P('seq', 'tensor'), may hold values from -6 to 6
- cache_keys: bfloat16 [32, 128, 3072], P('seq', None, 'tensor'), may hold values from -6 to 6
- cache_values: bfloat16 [32, 128, 3072], P('seq', None, 'tensor'), may hold values from -6 to 6
- hidden: bfloat16 [4096, 5120], P('seq', 'tensor'), may hold values from -6 to 6
- out_weight: bfloat16 [3072, 5120], P('seq', 'tensor'), may hold values from -0.21875 to 0.21875
- gate_table: float32 [1000, 5120], P(None, 'tensor'), may hold values from 0.3 to 2.5
- lengths: int32 [4], replicated, may hold values from 512 to 1536, as said below
- page_table: int32 [4, 4], replicated, may hold values from 0 to 31, as said below
- page_count: int32 [4], replicated, may hold values from 0 to 4
- timestep: int32 [4], replicated, may hold values from 0 to 999
Outputs:
- layer_out: bfloat16 [4096, 5120], P('seq', 'tensor')
Inputs may be any that keep to these rules, and one draw needn't show every extreme that they name: The lengths sum to 4096. `page_table`: a page named by clip c lies on a seq index that holds some token of clip c (page p lies on seq index p // 2); a page may be named by several clips or twice.
All inputs are finite; a program needn't handle non-finite values.
Results may differ from a plain program's by a relative error of at most 0.018.
Values may be sent and summed in bfloat16 or wider, within the bound.
A program may use at most 192 MiB of HBM per device.

v0:
```python
import math

import jax
import jax.numpy as jnp
from jax import lax
from jax.sharding import PartitionSpec as P

HD = 128
PAGE = 128
POOL = 2
REACH = 6


low_score = -1e30


def shifted(block, axis, distance):
    devices = range(lax.axis_size(axis))
    route = [(i - distance, i) for i in devices if i - distance in devices]
    return lax.ppermute(block, axis, route)


def clip_index(positions, clip_ends):
    return jnp.sum((positions[:, None] >= clip_ends[None, :]).astype(jnp.int32), axis=1)


def allowed_keys(query_clip, source, clip_ends, page_table, page_count, block_total, row_count):
    key_pos = source * row_count + jnp.arange(row_count, dtype=jnp.int32)
    in_range = (source >= 0) & (source < block_total)
    same_clip = (query_clip[:, None] == clip_index(key_pos, clip_ends)[None, :]) & in_range
    clip_total = clip_ends.shape[0]
    page_ids = source * POOL + jnp.arange(POOL, dtype=jnp.int32)
    live_slots = jnp.arange(page_table.shape[1], dtype=jnp.int32)[None, :] < page_count[:, None]
    named_pages = jnp.any(
        live_slots[:, :, None] & (page_table[:, :, None] == page_ids[None, None, :]), axis=1
    )
    member = query_clip[:, None] == jnp.arange(clip_total, dtype=jnp.int32)[None, :]
    page_ok = jnp.any(member[:, :, None] & named_pages[None], axis=1) & in_range
    page_ok = jnp.repeat(page_ok, PAGE, axis=1)
    return jnp.concatenate([same_clip, page_ok], axis=1)


def attend(carry_state, query_heads, key_heads, value_heads, allowed):
    running_max, totals, accumulated = carry_state
    scores = jnp.einsum(
        "qhd,khd->hqk", query_heads, key_heads, preferred_element_type=jnp.float32
    ) * (1.0 / math.sqrt(HD))
    scores = jnp.where(allowed[None], scores, low_score)
    new_max = jnp.maximum(running_max, jnp.max(scores, axis=2))
    factor = jnp.exp(running_max - new_max)
    weights = jnp.where(allowed[None], jnp.exp(scores - new_max[:, :, None]), 0.0)
    totals = totals * factor + jnp.sum(weights, axis=2)
    accumulated = accumulated * factor[:, :, None] + jnp.einsum(
        "hqk,khd->hqd",
        weights.astype(jnp.bfloat16),
        value_heads,
        preferred_element_type=jnp.float32,
    )
    return (new_max, totals, accumulated)


def empty_state(head_count, row_count):
    return (
        jnp.full((head_count, row_count), low_score, jnp.float32),
        jnp.zeros((head_count, row_count), jnp.float32),
        jnp.zeros((head_count, row_count, HD), jnp.float32),
    )


def visit_block(carry_state, packed, source, query_heads, query_clip, context):
    clip_ends, page_table, page_count, block_total = context
    row_count = query_heads.shape[0]
    head_count = query_heads.shape[1]
    allowed = allowed_keys(
        query_clip, source, clip_ends, page_table, page_count, block_total, row_count
    )
    key_heads = packed[0].reshape(-1, head_count, HD)
    value_heads = packed[1].reshape(-1, head_count, HD)
    return attend(carry_state, query_heads, key_heads, value_heads, allowed)


def fetch_direct(packed, offset):
    return shifted(packed, "seq", offset)


def local(
    queries,
    key_tiles,
    value_tiles,
    cache_keys,
    cache_values,
    hidden,
    out_weight,
    gate_table,
    lengths,
    page_table,
    page_count,
    timestep,
):
    row_count = queries.shape[0]
    tile_width = queries.shape[1]
    head_count = tile_width // HD
    block_total = lax.axis_size("seq")
    seq_index = lax.axis_index("seq")
    clip_ends = jnp.cumsum(lengths, dtype=jnp.int32)
    row_ids = jnp.arange(row_count, dtype=jnp.int32)
    positions = seq_index * row_count + row_ids
    query_clip = clip_index(positions, clip_ends)
    query_heads = queries.reshape(row_count, head_count, HD)
    context = (clip_ends, page_table, page_count, block_total)
    packed = jnp.stack(
        [
            jnp.concatenate([key_tiles, cache_keys.reshape(-1, tile_width)], axis=0),
            jnp.concatenate([value_tiles, cache_values.reshape(-1, tile_width)], axis=0),
        ]
    )
    carry_state = visit_block(
        empty_state(head_count, row_count), packed, seq_index, query_heads, query_clip, context
    )
    for offset in range(1, REACH + 1):
        from_below = fetch_direct(packed, offset)
        carry_state = visit_block(
            carry_state, from_below, seq_index - offset, query_heads, query_clip, context
        )
        from_above = fetch_direct(packed, -offset)
        carry_state = visit_block(
            carry_state, from_above, seq_index + offset, query_heads, query_clip, context
        )
    running_max, totals, accumulated = carry_state
    result = accumulated / totals[:, :, None]
    attention_local = (
        jnp.transpose(result, (1, 0, 2)).reshape(row_count, tile_width).astype(jnp.bfloat16)
    )
    attention = lax.all_gather(attention_local, "tensor", axis=1, tiled=True)
    projected = jnp.dot(
        attention,
        lax.all_gather(out_weight, "seq", axis=0, tiled=True),
        preferred_element_type=jnp.float32,
    )
    clip_total = lengths.shape[0]
    step_onehot = (
        timestep[:, None] == jnp.arange(gate_table.shape[0], dtype=jnp.int32)[None, :]
    ).astype(jnp.float32)
    clip_gate = jnp.dot(
        step_onehot, gate_table, precision=lax.Precision.HIGHEST, preferred_element_type=jnp.float32
    )
    clip_onehot = (query_clip[:, None] == jnp.arange(clip_total, dtype=jnp.int32)[None, :]).astype(
        jnp.float32
    )
    token_gate = jnp.dot(
        clip_onehot, clip_gate, precision=lax.Precision.HIGHEST, preferred_element_type=jnp.float32
    )
    return (hidden.astype(jnp.float32) + token_gate * projected).astype(jnp.bfloat16)


def solution(mesh):
    return jax.shard_map(
        local,
        mesh=mesh,
        in_specs=(
            P("seq", "tensor"),
            P("seq", "tensor"),
            P("seq", "tensor"),
            P("seq", None, "tensor"),
            P("seq", None, "tensor"),
            P("seq", "tensor"),
            P("seq", "tensor"),
            P(None, "tensor"),
            P(),
            P(),
            P(),
            P(),
        ),
        out_specs=P("seq", "tensor"),
        check_vma=False,
    )
```

profile of v0, /device:TPU:29, one launch (start us, length us, event | category | flops | bytes accessed | tf_op | source)
XLA Modules:
  0.0 803.2 jit_solution(7968295212195339989)
XLA Ops:
  9.4 2.3 copy.192
  14.6 1.9 pad_maximum_fusion
  17.7 6.6 collective-permute-start.11
  24.3 6.5 collective-permute-start.9
  32.1 3.0 collective-permute-start.7
  42.6 3.0 copy.109
  49.3 3.1 concatenate.64
  62.8 5.2 fusion
  68.0 20.6 %collective-permute-done.10 = bf16[2,512,1536]{1,2,0:T(8,128)(2,1)} collective-permute-done((bf16[2,512,1536]{1,2,0:T(8,128)(2,1)}, bf16[2,512,1536]{1,2,0:T(8,128)(2,1)}, u32[]{:S(2)}, u32[]{:S(2)}) %collective-permute-start.10) | collective-permute-done | bytes 3145760 | tf_op jit(solution)/shard_map/ppermute | solution.py:20
  89.8 2.1 fusion.177
  93.2 74.6 %collective-permute-done.11 = bf16[2,512,1536]{1,2,0:T(8,128)(2,1)} collective-permute-done((bf16[2,512,1536]{1,2,0:T(8,128)(2,1)}, bf16[2,512,1536]{1,2,0:T(8,128)(2,1)}, u32[]{:S(2)}, u32[]{:S(2)}) %collective-permute-start.11) | collective-permute-done | bytes 3145760 | tf_op jit(solution)/shard_map/ppermute | solution.py:20
  167.8 14.7 %collective-permute-start.5 = (bf16[2,512,1536]{1,2,0:T(8,128)(2,1)}, bf16[2,512,1536]{1,2,0:T(8,128)(2,1)S(1)}, u32[]{:S(2)}, u32[]{:S(2)}) collective-permute-start(bf16[2,512,1536]{1,2,0:T(8,128)(2,1)} %pad_maximum_fusion), channel_id=1, source_target_pairs={{6,0},{8,2},{10,4},{12,6},{14,8},{16,10},{18,12},{20,14},{22,16},{... | collective-permute-start | bytes 9437192 | tf_op jit(solution)/shard_map/ppermute | solution.py:20
  182.6 3.2 fusion.166
  187.1 48.4 %collective-permute-done.9 = bf16[2,512,1536]{1,2,0:T(8,128)(2,1)} collective-permute-done((bf16[2,512,1536]{1,2,0:T(8,128)(2,1)}, bf16[2,512,1536]{1,2,0:T(8,128)(2,1)}, u32[]{:S(2)}, u32[]{:S(2)}) %collective-permute-start.9) | collective-permute-done | bytes 3145760 | tf_op jit(solution)/shard_map/ppermute | solution.py:20
  235.5 1.5 collective-permute-start.4
  237.0 2.1 fusion.176
  240.4 2.9 collective-permute-start.3
  243.4 2.1 fusion.175
  246.8 56.1 %collective-permute-done.7 = bf16[2,512,1536]{1,2,0:T(8,128)(2,1)} collective-permute-done((bf16[2,512,1536]{1,2,0:T(8,128)(2,1)}, bf16[2,512,1536]{1,2,0:T(8,128)(2,1)}, u32[]{:S(2)}, u32[]{:S(2)}) %collective-permute-start.7) | collective-permute-done | bytes 3145760 | tf_op jit(solution)/shard_map/ppermute | solution.py:20
  304.2 3.3 fusion.174
  307.4 3.9 fusion.8
  311.4 5.3 collective-permute-start.1
  318.0 3.9 fusion.7
  324.6 3.9 fusion.6
  328.5 3.3 fusion.171
  331.7 4.0 fusion.5
  335.8 108.8 %collective-permute-done.3 = bf16[2,512,1536]{1,2,0:T(8,128)(2,1)} collective-permute-done((bf16[2,512,1536]{1,2,0:T(8,128)(2,1)}, bf16[2,512,1536]{1,2,0:T(8,128)(2,1)}, u32[]{:S(2)}, u32[]{:S(2)}) %collective-permute-start.3) | collective-permute-done | bytes 3145760 | tf_op jit(solution)/shard_map/ppermute | solution.py:20
  444.6 3.2 fusion.170
  447.8 4.0 fusion.4
  451.8 3.3 fusion.169
  455.0 3.9 fusion.3
  459.0 3.2 fusion.168
  462.2 3.9 fusion.2
  467.4 3.9 fusion.1
  471.3 1.5 fusion.35
  472.9 10.5 %fusion.43 = f32[12,256,128]{1,2,0:T(8,128)S(1)} fusion(bf16[512,12,128]{0,2,1:T(8,128)(2,1)S(1)} %bitcast.554, f32[12,512,256]{2,1,0:T(8,128)S(1)} %get-tuple-element.115, f32[12,256]{1,0:T(8,128)S(1)} %get-tuple-element.61, pred[256,512]{0,1:T(8,128)(4,1)S(1)} %copy-done.11), kind=kOutput, calls=%fused_computation.70 | convolution fusion | flops 410517504 | bytes 9580544 | tf_op jit(solution)/shard_map/hqk,khd->hqd/dot_general | solution.py:53
  483.4 1.5 fusion.33
  484.9 1.7 fusion.45
  486.7 1.5 fusion.31
  488.2 1.7 fusion.47
  490.0 1.5 fusion.29
  491.5 1.7 fusion.49
  495.0 1.9 fusion.51
  497.0 1.5 fusion.25
  498.5 2.9 fusion.53
  501.4 1.5 fusion.23
  503.0 2.9 fusion.55
  505.9 1.5 fusion.21
  507.4 2.9 fusion.57
  510.3 1.5 fusion.19
  511.9 3.3 fusion.59
  515.2 1.5 fusion.17
  516.7 2.9 fusion.61
  519.6 1.5 fusion.15
  521.1 2.9 fusion.63
  524.0 1.5 fusion.13
  525.5 2.9 fusion.65
  528.4 1.5 fusion.37
  530.2 7.3 fusion.88
  538.3 7.2 fusion.119
  545.5 119.8 %all-gather.3.cloned.1.call-done = bf16[256,3072]{0,1:T(8,128)(2,1)} async-done(((bf16[256,1536]{0,1:T(8,128)(2,1)}), bf16[256,3072]{0,1:T(8,128)(2,1)}) %all-gather.3.cloned.1.call-update) | async-done | bytes 1572880 | tf_op jit(solution)/shard_map/all_gather | solution.py:134
  665.3 120.1 %all-gather.5.cloned.1.call-done = bf16[3072,2560]{1,0:T(8,128)(2,1)} async-done(((bf16[192,2560]{1,0:T(8,128)(2,1)}), bf16[3072,2560]{1,0:T(8,128)(2,1)}) %all-gather.5.cloned.1.call-update) | async-done | bytes 15728656 | tf_op jit(solution)/shard_map/all_gather | solution.py:137
  785.4 8.2 %fusion.178 = f32[256,2560]{1,0:T(8,128)S(1)} fusion(bf16[256,3072]{0,1:T(8,128)(2,1)} %all-gather.3.cloned.1.call-done, bf16[3072,2560]{1,0:T(8,128)(2,1)} %all-gather.5.cloned.1.call-done), kind=kOutput, calls=%fused_computation.349 | convolution fusion | flops 4026531840 | bytes 19922944 | tf_op jit(solution)/shard_map/dot_general | solution.py:135
  793.7 2.5 fusion.40
  (181 shorter events, 45.6 us)
Async XLA Ops:
  6.5 658.7 %all-gather.3.cloned.1.call-start = ((), (), s32[]{:S(2)}) async-start(), calls=%async_computation | async-start | bytes 2359296 | tf_op jit(solution)/shard_map/all_gather | solution.py:134
  13.0 22.1 %copy-start.18 = (s32[4]{0:T(128)S(1)}, s32[4]{0:T(128)}, u32[]{:S(2)}) copy-start(s32[4]{0:T(128)} %param.22) | copy-start | bytes 52
  13.1 22.1 %copy-start.19 = (s32[4]{0:T(128)S(1)}, s32[4]{0:T(128)}, u32[]{:S(2)}) copy-start(s32[4]{0:T(128)} %param.20) | copy-start | bytes 52
  13.1 22.6 %copy-start.16 = (s32[4,4]{1,0:T(4,128)S(1)}, s32[4,4]{1,0:T(4,128)}, u32[]{:S(2)}) copy-start(s32[4,4]{1,0:T(4,128)} %param.21) | copy-start | bytes 196
  13.1 28.9 %copy-start = (bf16[2,128,1536]{2,1,0:T(8,128)(2,1)S(1)}, bf16[2,128,1536]{2,1,0:T(8,128)(2,1)}, u32[]{:S(2)}) copy-start(bf16[2,128,1536]{2,1,0:T(8,128)(2,1)} %param.15) | copy-start | bytes 2359300
  16.5 72.1 %collective-permute-start.10 = (bf16[2,512,1536]{1,2,0:T(8,128)(2,1)}, bf16[2,512,1536]{1,2,0:T(8,128)(2,1)}, u32[]{:S(2)}, u32[]{:S(2)}) collective-permute-start(bf16[2,512,1536]{1,2,0:T(8,128)(2,1)} %pad_maximum_fusion), channel_id=1, source_target_pairs={{0,12},{2,14},{4,16},{6,18},{8,20},{10,22},{12,24},{14,26},{16,28}... | collective-permute-start | bytes 9437192 | tf_op jit(solution)/shard_map/ppermute | solution.py:20
  17.7 150.1 %collective-permute-start.11 = (bf16[2,512,1536]{1,2,0:T(8,128)(2,1)}, bf16[2,512,1536]{1,2,0:T(8,128)(2,1)}, u32[]{:S(2)}, u32[]{:S(2)}) collective-permute-start(bf16[2,512,1536]{1,2,0:T(8,128)(2,1)} %pad_maximum_fusion), channel_id=1, source_target_pairs={{12,0},{14,2},{16,4},{18,6},{20,8},{22,10},{24,12},{26,14},{28,16}... | collective-permute-start | bytes 9437192 | tf_op jit(solution)/shard_map/ppermute | solution.py:20
  24.3 211.2 %collective-permute-start.9 = (bf16[2,512,1536]{1,2,0:T(8,128)(2,1)}, bf16[2,512,1536]{1,2,0:T(8,128)(2,1)}, u32[]{:S(2)}, u32[]{:S(2)}) collective-permute-start(bf16[2,512,1536]{1,2,0:T(8,128)(2,1)} %pad_maximum_fusion), channel_id=1, source_target_pairs={{10,0},{12,2},{14,4},{16,6},{18,8},{20,10},{22,12},{24,14},{26,16}... | collective-permute-start | bytes 9437192 | tf_op jit(solution)/shard_map/ppermute | solution.py:20
  30.8 209.6 %collective-permute-start.8 = (bf16[2,512,1536]{1,2,0:T(8,128)(2,1)}, bf16[2,512,1536]{1,2,0:T(8,128)(2,1)}, u32[]{:S(2)}, u32[]{:S(2)}) collective-permute-start(bf16[2,512,1536]{1,2,0:T(8,128)(2,1)} %pad_maximum_fusion), channel_id=1, source_target_pairs={{0,10},{2,12},{4,14},{6,16},{8,18},{10,20},{12,22},{14,24},{16,26}... | collective-permute-start | bytes 9437192 | tf_op jit(solution)/shard_map/ppermute | solution.py:20
  32.1 270.7 %collective-permute-start.7 = (bf16[2,512,1536]{1,2,0:T(8,128)(2,1)}, bf16[2,512,1536]{1,2,0:T(8,128)(2,1)}, u32[]{:S(2)}, u32[]{:S(2)}) collective-permute-start(bf16[2,512,1536]{1,2,0:T(8,128)(2,1)} %pad_maximum_fusion), channel_id=1, source_target_pairs={{8,0},{10,2},{12,4},{14,6},{16,8},{18,10},{20,12},{22,14},{24,16},... | collective-permute-start | bytes 9437192 | tf_op jit(solution)/shard_map/ppermute | solution.py:20
  62.8 29.1 %copy-start.11 = (pred[256,512]{0,1:T(8,128)(4,1)S(1)}, pred[256,512]{0,1:T(8,128)(4,1)}, u32[]{:S(2)}) copy-start(pred[256,512]{0,1:T(8,128)(4,1)} %pad_add_fusion.11) | copy-start | bytes 393220
  88.5 222.9 %collective-permute-start.6 = (bf16[2,512,1536]{1,2,0:T(8,128)(2,1)}, bf16[2,512,1536]{1,2,0:T(8,128)(2,1)S(1)}, u32[]{:S(2)}, u32[]{:S(2)}) collective-permute-start(bf16[2,512,1536]{1,2,0:T(8,128)(2,1)} %pad_maximum_fusion), channel_id=1, source_target_pairs={{0,8},{2,10},{4,12},{6,14},{8,16},{10,18},{12,20},{14,22},{16,24},... | collective-permute-start | bytes 9437192 | tf_op jit(solution)/shard_map/ppermute | solution.py:20
  167.8 154.1 %collective-permute-start.5 = (bf16[2,512,1536]{1,2,0:T(8,128)(2,1)}, bf16[2,512,1536]{1,2,0:T(8,128)(2,1)S(1)}, u32[]{:S(2)}, u32[]{:S(2)}) collective-permute-start(bf16[2,512,1536]{1,2,0:T(8,128)(2,1)} %pad_maximum_fusion), channel_id=1, source_target_pairs={{6,0},{8,2},{10,4},{12,6},{14,8},{16,10},{18,12},{20,14},{22,16},{... | collective-permute-start | bytes 9437192 | tf_op jit(solution)/shard_map/ppermute | solution.py:20
  185.8 53.3 %copy-start.12 = (pred[256,512]{0,1:T(8,128)(4,1)S(1)}, pred[256,512]{0,1:T(8,128)(4,1)}, u32[]{:S(2)}) copy-start(pred[256,512]{0,1:T(8,128)(4,1)} %pad_add_fusion.10) | copy-start | bytes 393220
  235.5 93.0 %collective-permute-start.4 = (bf16[2,512,1536]{1,2,0:T(8,128)(2,1)}, bf16[2,512,1536]{1,2,0:T(8,128)(2,1)}, u32[]{:S(2)}, u32[]{:S(2)}) collective-permute-start(bf16[2,512,1536]{1,2,0:T(8,128)(2,1)} %pad_maximum_fusion), channel_id=1, source_target_pairs={{0,6},{2,8},{4,10},{6,12},{8,14},{10,16},{12,18},{14,20},{16,22},{... | collective-permute-start | bytes 9437192 | tf_op jit(solution)/shard_map/ppermute | solution.py:20
  239.1 6.4 copy-start.14
  240.4 204.1 %collective-permute-start.3 = (bf16[2,512,1536]{1,2,0:T(8,128)(2,1)}, bf16[2,512,1536]{1,2,0:T(8,128)(2,1)}, u32[]{:S(2)}, u32[]{:S(2)}) collective-permute-start(bf16[2,512,1536]{1,2,0:T(8,128)(2,1)} %pad_maximum_fusion), channel_id=1, source_target_pairs={{4,0},{6,2},{8,4},{10,6},{12,8},{14,10},{16,12},{18,14},{20,16},{2... | collective-permute-start | bytes 9437192 | tf_op jit(solution)/shard_map/ppermute | solution.py:20
  245.5 62.0 %copy-start.13 = (pred[256,512]{0,1:T(8,128)(4,1)S(1)}, pred[256,512]{0,1:T(8,128)(4,1)}, u32[]{:S(2)}) copy-start(pred[256,512]{0,1:T(8,128)(4,1)} %pad_add_fusion.8) | copy-start | bytes 393220
  302.9 148.9 %collective-permute-start.2 = (bf16[2,512,1536]{1,2,0:T(8,128)(2,1)}, bf16[2,512,1536]{1,2,0:T(8,128)(2,1)}, u32[]{:S(2)}, u32[]{:S(2)}) collective-permute-start(bf16[2,512,1536]{1,2,0:T(8,128)(2,1)} %pad_maximum_fusion), channel_id=1, source_target_pairs={{0,4},{2,6},{4,8},{6,10},{8,12},{10,14},{12,16},{14,18},{16,20},{1... | collective-permute-start | bytes 9437192 | tf_op jit(solution)/shard_map/ppermute | solution.py:20
  311.4 147.6 %collective-permute-start.1 = (bf16[2,512,1536]{1,2,0:T(8,128)(2,1)}, bf16[2,512,1536]{1,2,0:T(8,128)(2,1)}, u32[]{:S(2)}, u32[]{:S(2)}) collective-permute-start(bf16[2,512,1536]{1,2,0:T(8,128)(2,1)} %pad_maximum_fusion), channel_id=1, source_target_pairs={{2,0},{4,2},{6,4},{8,6},{10,8},{12,10},{14,12},{16,14},{18,16},{20... | collective-permute-start | bytes 9437192 | tf_op jit(solution)/shard_map/ppermute | solution.py:20
  321.9 144.1 %collective-permute-start = (bf16[2,512,1536]{1,2,0:T(8,128)(2,1)}, bf16[2,512,1536]{1,2,0:T(8,128)(2,1)S(1)}, u32[]{:S(2)}, u32[]{:S(2)}) collective-permute-start(bf16[2,512,1536]{1,2,0:T(8,128)(2,1)} %pad_maximum_fusion), channel_id=1, source_target_pairs={{0,2},{2,4},{4,6},{6,8},{8,10},{10,12},{12,14},{14,16},{16,18},{18... | collective-permute-start | bytes 9437192 | tf_op jit(solution)/shard_map/ppermute | solution.py:20
  486.7 3.3 slice-start
  488.2 1.8 slice-start.1
  489.9 1.6 copy-start.2
  490.0 3.3 slice-start.2
  491.5 2.0 slice-start.3
  493.2 1.7 copy-start.3
  493.5 3.5 slice-start.4
  495.0 2.0 slice-start.5
  496.9 1.6 copy-start.4
  497.0 4.5 slice-start.6
  498.5 2.9 slice-start.7
  501.4 1.5 copy-start.5
  501.4 4.5 slice-start.8
  503.0 2.9 slice-start.9
  505.9 1.5 copy-start.6
  505.9 4.4 slice-start.10
  507.4 2.9 slice-start.11
  510.3 1.5 copy-start.7
  510.3 4.8 slice-start.12
  511.8 3.3 slice-start.13
  515.1 1.5 copy-start.8
  515.1 4.4 slice-start.14
  516.7 2.9 slice-start.15
  519.6 1.5 copy-start.9
  519.6 4.4 slice-start.16
  521.1 2.9 slice-start.17
  524.0 1.5 copy-start.15
  528.4 1.8 copy-start.1
  530.2 8.1 %copy-start.17 = (s32[4]{0:T(128)S(1)}, s32[4]{0:T(128)}, u32[]{:S(2)}) copy-start(s32[4]{0:T(128)} %param.23) | copy-start | bytes 52
  537.6 247.8 %all-gather.5.cloned.1.call-start = ((), (), s32[]{:S(2)}) async-start(), calls=%async_computation.1 | async-start | bytes 16711680 | tf_op jit(solution)/shard_map/all_gather | solution.py:137
  545.5 248.1 %copy-start.10 = (bf16[256,2560]{1,0:T(8,128)(2,1)S(1)}, bf16[256,2560]{1,0:T(8,128)(2,1)}, u32[]{:S(2)}) copy-start(bf16[256,2560]{1,0:T(8,128)(2,1)} %param.17) | copy-start | bytes 3932164
Sparse Core Ops, SparseCore 0:
  537.7 127.5 all-gather.2
  667.6 117.7 all-gather.4
where the time goes:
time: 813 us; the launch traced here: 803 us
  waiting for transfers between devices  549 us (68%)
  matrix products  105 us (13%)
  local copies, waits for them, and re-layouts  47.4 us (6%)
  starting transfers between devices  47 us (6%)
  other arithmetic  40.1 us (5%)
  between operations  14.5 us (2%)
    ppermute x12, waiting for transfers between devices, shifted(): return lax.ppermute(block, axis, route)  308 us
    all_gather x1, waiting for transfers between devices, local(): lax.all_gather(out_weight, 'seq', axis=0, tiled=True)  120 us
    all_gather x1, waiting for transfers between devices, local(): attention = lax.all_gather(attention_local, 'tensor', axis=1, tiled=True)  120 us
    ppermute x12, starting transfers between devices, shifted(): return lax.ppermute(block, axis, route)  47 us
    dot_general x13, matrix products, attend(): jnp.einsum('hqk,khd->hqd', weights.astype(jnp.bfloat16), value_heads, pre...  45.5 us
    dot_general x13, matrix products, attend(): jnp.einsum('qhd,khd->hqk', query_heads, key_heads, preferred_element_type...  41.7 us
    slice x11, local copies, waits for them, and re-layouts, visit_block(): value_heads = packed[1].reshape(-1, head_count, HD)  27.7 us
    reduce_sum x13, other arithmetic, attend(): totals = totals * factor + jnp.sum(weights, axis=2)  19.6 us
  transfers between devices with their start and end apart: 14, of which 7 were waited for; matrix products, arithmetic and copies ran while one was open for 13% of the time, Pallas kernels for 0%

commit v1 on v0

v1 whole, which is shorter than its diff:
```python
import functools
import math

import jax
import jax.numpy as jnp
from jax import lax
from jax.experimental import pallas as pl
from jax.experimental.pallas import tpu as pltpu
from jax.sharding import PartitionSpec as P

HD = 128
PAGE = 128
POOL = 2
REACH = 6

MESH = pl.DeviceIdType.MESH
ANY = pl.BlockSpec(memory_space=pl.ANY)
VMEM = pl.BlockSpec(memory_space=pltpu.VMEM)
SMEM = pl.BlockSpec(memory_space=pltpu.SMEM)
SCALE = math.log2(math.e) / math.sqrt(HD)


def owner_of(head, heads, n):
    return lax.div(head * n, heads)


def owned_by(index, heads, n):
    head = lax.div(index * heads + n - 1, n)
    return (head < heads) & (owner_of(head, heads, n) == index), head


def greet_seq(n, me, tensor):
    barrier = pltpu.get_barrier_semaphore()

    def signal(step, carry):
        peer = (me + step) % n
        pl.semaphore_signal(barrier, inc=1, device_id=(peer, tensor), device_id_type=MESH)
        return carry

    lax.fori_loop(1, n, signal, 0)
    return barrier


def scatter_heads(n, heads, q, k, v, ck, cv, out, send_sem, recv_sem):
    me, tensor = lax.axis_index("seq"), lax.axis_index("tensor")
    barrier = greet_seq(n, me, tensor)
    pl.semaphore_wait(barrier, n - 1)
    mine, _ = owned_by(me, heads, n)

    def send(step, carry):
        head = (step + me) % heads
        owner = owner_of(head, heads, n)
        columns = pl.ds(pl.multiple_of(head * HD, HD), HD)

        @pl.when(owner == me)
        def _():
            for a, ref in enumerate((q, k, v, ck, cv)):
                pltpu.make_async_copy(ref.at[:, columns], out.at[a, me], recv_sem.at[a]).start()

        @pl.when(owner != me)
        def _():
            for a, ref in enumerate((q, k, v, ck, cv)):
                pltpu.make_async_remote_copy(
                    src_ref=ref.at[:, columns],
                    dst_ref=out.at[a, me],
                    send_sem=send_sem.at[a],
                    recv_sem=recv_sem.at[a],
                    device_id=(owner, tensor),
                    device_id_type=MESH,
                ).start()

        return carry

    lax.fori_loop(0, heads, send, 0)

    @pl.when(mine)
    def _():
        for a, ref in enumerate((q, k, v, ck, cv)):
            pltpu.make_async_copy(out.at[a], out.at[a], recv_sem.at[a]).wait()
            if heads > 1:
                part = ref.at[:, pl.ds(0, (heads - 1) * HD)]
                pltpu.make_async_copy(part, part, send_sem.at[a]).wait()

    @pl.when(jnp.logical_not(mine))
    def _():
        for a, ref in enumerate((q, k, v, ck, cv)):
            pltpu.make_async_copy(ref, ref, send_sem.at[a]).wait()


def attend_head(n, heads, rows, window, clips, slots, lengths, page_table, page_count, r, out, scores):
    contract = (((1,), (1,)), ((), ()))

    def item(c, block, start, end, base, token_blocks, page_pairs):
        query = r[0, block]
        chunks = []
        for j in range(token_blocks):
            position = (base + j) * rows + lax.broadcasted_iota(jnp.int32, (1, rows), 1)
            ok = (position >= start) & (position < end)
            chunks.append((r[1, base + j], r[2, base + j], ok))
        count = page_count[c]
        lane = lax.broadcasted_iota(jnp.int32, (1, 2 * PAGE), 1)
        for pair in range(page_pairs):
            keys, values, live = [], [], []
            for slot in (2 * pair, 2 * pair + 1):
                real = min(slot, slots - 1)
                page = page_table[c, real]
                alive = jnp.int32(slot) < count
                if slot >= slots:
                    alive = alive & False
                for before in range(real):
                    alive = alive & (page_table[c, before] != page)
                owner = page // POOL
                offset = pl.ds(pl.multiple_of((page % POOL) * PAGE, PAGE), PAGE)
                keys.append(r[3, owner, offset])
                values.append(r[4, owner, offset])
                live.append(alive.astype(jnp.int32))
            ok = jnp.where(lane < PAGE, live[0], live[1]) > 0
            chunks.append(
                (jnp.concatenate(keys, axis=0), jnp.concatenate(values, axis=0), ok)
            )
        top = None
        width = chunks[0][0].shape[0]
        for j, (key, _, ok) in enumerate(chunks):
            s = lax.dot_general(query, key, contract, preferred_element_type=jnp.float32)
            s = s * SCALE + jnp.where(ok, 0.0, -1e30)
            scores[:, j * width : (j + 1) * width] = s
            part = jnp.maximum(s[:, :HD], s[:, HD:])
            top = part if top is None else jnp.maximum(top, part)
        top = jnp.max(top, axis=1, keepdims=True)
        total = None
        for j, (_, value, _) in enumerate(chunks):
            weight = jnp.exp2(scores[:, j * width : (j + 1) * width] - top).astype(jnp.bfloat16)
            wide = jnp.concatenate([value, jnp.ones_like(value)], axis=1)
            add = jnp.dot(weight, wide, preferred_element_type=jnp.float32)
            total = add if total is None else total + add
        result = (total[:, :HD] / total[:, HD:]).astype(jnp.bfloat16)
        position = block * rows + lax.broadcasted_iota(jnp.int32, (rows, HD), 0)
        inside = (position >= start) & (position < end)
        out[block] = jnp.where(inside, result, out[block])

    mine, _ = owned_by(lax.axis_index("seq"), heads, n)

    @pl.when(mine)
    def _():
        def clip_step(c, start):
            end = start + lengths[c]
            first = start // rows
            last = (end - 1) // rows
            span = last - first + 1
            count = page_count[c]
            pairs = (slots + 1) // 2
            small = min((window + 1) // 2, window)

            def run(token_blocks, page_pairs):
                base = jnp.minimum(first, n - token_blocks)

                def step(block, carry):
                    item(c, block, start, end, base, token_blocks, page_pairs)
                    return carry

                lax.fori_loop(first, last + 1, step, 0)

            for token_blocks, fits in ((small, span <= small), (window, span > small)):
                for page_pairs, named in ((0, count <= 0), (pairs, count > 0)):
                    pl.when(fits & named)(functools.partial(run, token_blocks, page_pairs))
            return end

        lax.fori_loop(0, clips, clip_step, jnp.int32(0))


def return_heads(n, tensors, heads, att, out, send_sem, recv_sem, pass_sem, land_sem):
    me, tensor = lax.axis_index("seq"), lax.axis_index("tensor")
    barrier = greet_seq(n, me, tensor)

    def greet(step, carry):
        peer = (tensor + step) % tensors
        pl.semaphore_signal(barrier, inc=1, device_id=(me, peer), device_id_type=MESH)
        return carry

    lax.fori_loop(1, tensors, greet, 0)
    pl.semaphore_wait(barrier, n - 1 + tensors - 1)
    mine, my_head = owned_by(me, heads, n)

    def place(head, side):
        return out.at[:, pl.ds(pl.multiple_of((side * heads + head) * HD, HD), HD)]

    @pl.when(mine)
    def _():
        def send(step, carry):
            peer = (me + step) % n
            pltpu.make_async_remote_copy(
                src_ref=att.at[peer],
                dst_ref=place(my_head, tensor),
                send_sem=send_sem.at[0],
                recv_sem=recv_sem.at[my_head],
                device_id=(peer, tensor),
                device_id_type=MESH,
            ).start()
            return carry

        lax.fori_loop(1, n, send, 0)
        pltpu.make_async_copy(att.at[me], place(my_head, tensor), recv_sem.at[my_head]).start()

    def relay(step, carry):
        head = step
        here = place(head, tensor)
        pltpu.make_async_copy(here, here, recv_sem.at[head]).wait()

        def pass_on(other, inner):
            peer = (tensor + other) % tensors
            pltpu.make_async_remote_copy(
                src_ref=here,
                dst_ref=here,
                send_sem=pass_sem.at[head],
                recv_sem=land_sem.at[tensor, head],
                device_id=(me, peer),
                device_id_type=MESH,
            ).start()
            return inner

        lax.fori_loop(1, tensors, pass_on, 0)
        return carry

    lax.fori_loop(0, heads, relay, 0)

    def finish(step, carry):
        def land(other, inner):
            peer = (tensor + other) % tensors
            there = place(step, peer)
            pltpu.make_async_copy(there, there, land_sem.at[peer, step]).wait()
            mine_here = place(step, tensor)
            pltpu.make_async_copy(mine_here, mine_here, pass_sem.at[step]).wait()
            return inner

        return lax.fori_loop(1, tensors, land, carry)

    lax.fori_loop(0, heads, finish, 0)

    @pl.when(mine)
    def _():
        part = att.at[pl.ds(0, n - 1)]
        pltpu.make_async_copy(part, part, send_sem.at[0]).wait()


def clip_index(positions, clip_ends):
    return jnp.sum((positions[:, None] >= clip_ends[None, :]).astype(jnp.int32), axis=1)


def local(
    n,
    tensors,
    queries,
    key_tiles,
    value_tiles,
    cache_keys,
    cache_values,
    hidden,
    out_weight,
    gate_table,
    lengths,
    page_table,
    page_count,
    timestep,
):
    rows, tile_width = queries.shape
    heads = tile_width // HD
    clips, slots = page_table.shape
    seq_index = lax.axis_index("seq")
    window = min(REACH + 1, n)
    pairs = (slots + 1) // 2

    weight = lax.all_gather(out_weight, "seq", axis=0, tiled=True)

    received = pl.pallas_call(
        functools.partial(scatter_heads, n, heads),
        out_shape=jax.ShapeDtypeStruct((5, n, rows, HD), jnp.bfloat16),
        in_specs=[ANY] * 5,
        out_specs=ANY,
        scratch_shapes=[pltpu.SemaphoreType.DMA((5,)), pltpu.SemaphoreType.DMA((5,))],
        compiler_params=pltpu.CompilerParams(collective_id=0, has_side_effects=True),
        cost_estimate=pl.CostEstimate(flops=0, bytes_accessed=200_000_000, transcendentals=0),
        name="scatter_heads",
    )(
        queries,
        key_tiles,
        value_tiles,
        cache_keys.reshape(rows, tile_width),
        cache_values.reshape(rows, tile_width),
    )

    attended = pl.pallas_call(
        functools.partial(attend_head, n, heads, rows, window, clips, slots),
        out_shape=jax.ShapeDtypeStruct((n, rows, HD), jnp.bfloat16),
        in_specs=[SMEM] * 3 + [VMEM],
        out_specs=VMEM,
        scratch_shapes=[pltpu.VMEM((rows, (window + pairs) * rows), jnp.float32)],
        compiler_params=pltpu.CompilerParams(vmem_limit_bytes=50 * 1024 * 1024),
        cost_estimate=pl.CostEstimate(
            flops=4 * n * rows * window * rows * HD,
            bytes_accessed=6 * n * rows * HD * 2,
            transcendentals=n * rows * window * rows,
        ),
        name="attend_head",
    )(lengths, page_table, page_count, received)

    attention = pl.pallas_call(
        functools.partial(return_heads, n, tensors, heads),
        out_shape=jax.ShapeDtypeStruct((rows, tensors * tile_width), jnp.bfloat16),
        in_specs=[ANY],
        out_specs=ANY,
        scratch_shapes=[
            pltpu.SemaphoreType.DMA((1,)),
            pltpu.SemaphoreType.DMA((heads,)),
            pltpu.SemaphoreType.DMA((heads,)),
            pltpu.SemaphoreType.DMA((tensors, heads)),
        ],
        compiler_params=pltpu.CompilerParams(collective_id=1, has_side_effects=True),
        cost_estimate=pl.CostEstimate(flops=0, bytes_accessed=80_000_000, transcendentals=0),
        name="return_heads",
    )(attended)

    projected = jnp.dot(attention, weight, preferred_element_type=jnp.float32)
    clip_ends = jnp.cumsum(lengths, dtype=jnp.int32)
    positions = seq_index * rows + jnp.arange(rows, dtype=jnp.int32)
    query_clip = clip_index(positions, clip_ends)
    gates = [
        lax.dynamic_slice_in_dim(gate_table, timestep[c], 1, 0) for c in range(clips)
    ]
    token_gate = gates[0]
    for c in range(1, clips):
        token_gate = jnp.where(query_clip[:, None] == c, gates[c], token_gate)
    return (hidden.astype(jnp.float32) + token_gate * projected).astype(jnp.bfloat16)


def solution(mesh):
    return jax.shard_map(
        functools.partial(local, mesh.shape["seq"], mesh.shape["tensor"]),
        mesh=mesh,
        in_specs=(
            P("seq", "tensor"),
            P("seq", "tensor"),
            P("seq", "tensor"),
            P("seq", None, "tensor"),
            P("seq", None, "tensor"),
            P("seq", "tensor"),
            P("seq", "tensor"),
            P(None, "tensor"),
            P(),
            P(),
            P(),
            P(),
        ),
        out_specs=P("seq", "tensor"),
        check_vma=False,
    )
```

time: 813 us -> 258 us (0.32); the launches traced: 803 us -> 258 us
  waiting for transfers between devices: 549 us -> 0.72 us
  Pallas kernels: 0 us -> 220 us
  matrix products: 105 us -> 11.6 us
  starting transfers between devices: 47 us -> 0.01 us
  local copies, waits for them, and re-layouts: 47.4 us -> 3.54 us
  other arithmetic: 40.1 us -> 0.93 us
    ppermute x12 -> x0, waiting for transfers between devices: 308 us -> none  [shifted(): return lax.ppermute(block, axis, route)]
    all_gather x2 -> x1, waiting for transfers between devices: 240 us -> 0.01 us  [local(): weight = lax.all_gather(out_weight, 'seq', axis=0, tiled=True)]
    pallas_call x0 -> x3, Pallas kernels: none -> 220 us  [the longest x1 121 us: local(): pl.pallas_call(functools.partial(return_heads, n, tensors, heads), out_sh...]
    dot_general x29 -> x1, matrix products: 105 us -> 11.6 us  [local(): projected = jnp.dot(attention, weight, preferred_element_type=jnp.float32)]
    ppermute x12 -> x0, starting transfers between devices: 47 us -> none  [shifted(): return lax.ppermute(block, axis, route)]
    slice x12 -> x1, local copies, waits for them, and re-layouts: 29.8 us -> 1.43 us  [local(): timestep[c]]
    reduce_sum x13 -> x0, other arithmetic: 19.6 us -> none  [attend(): totals = totals * factor + jnp.sum(weights, axis=2)]
    concatenate x13 -> x0, other arithmetic: 9.46 us -> none  [allowed_keys(): return jnp.concatenate([same_clip, page_ok], axis=1)]
  transfers between devices with their start and end apart: 14 -> 1, of which waited for: 7 -> 0; matrix products, arithmetic and copies ran while one was open for 13% -> 1% of each run, Pallas kernels for 0% -> 85%
where the time goes in v1:
time: 258 us
  Pallas kernels  220 us (85%)
  between operations  20.9 us (8%)
  matrix products  11.6 us (4%)
  local copies, waits for them, and re-layouts  3.54 us (1%)
    pallas_call x1, Pallas kernels, local(): pl.pallas_call(functools.partial(return_heads, n, tensors, heads), out_sh...  121 us
    pallas_call x1, Pallas kernels, local(): pl.pallas_call(functools.partial(scatter_heads, n, heads), out_shape=jax....  96.2 us
    dot_general x1, matrix products, local(): projected = jnp.dot(attention, weight, preferred_element_type=jnp.float32)  11.6 us
  transfers between devices with their start and end apart: 1, of which 0 were waited for; matrix products, arithmetic and copies ran while one was open for 1% of the time, Pallas kernels for 85%

profile of v1, /device:TPU:29, one launch (start us, length us, event | category | flops | bytes accessed | tf_op | source)
XLA Modules:
  0.0 257.7 jit_solution(17025640802384658809)
XLA Ops:
  6.5 0.0 all-gather.2.cloned.1.call-start
  6.5 0.7 all-gather.2.cloned.1.call-update
  7.3 1.4 fusion.2
  13.6 0.8 reduce-window.8
  14.5 0.0 copy-start.1
  14.5 0.0 copy-start.2
  14.5 0.0 copy-start.3
  14.5 96.2 %scatter_heads.1.r = bf16[5,16,256,128]{3,2,1,0:T(8,128)(2,1)} custom-call(bf16[256,1536]{1,0:T(8,128)(2,1)} %q.1, bf16[256,1536]{1,0:T(8,128)(2,1)} %k.1, bf16[256,1536]{1,0:T(8,128)(2,1)} %v.1, bf16[256,1536]{1,0:T(8,128)(2,1)} %bitcast.11, bf16[256,1536]{1,0:T(8,128)(2,1)} %bitcast.12), custom_call_target="tpu_custom_call" | custom-call | bytes 200000000 | tf_op jit(solution)/shard_map/scatter_heads/pallas_call | solution.py:274
  110.7 0.0 copy-done.1
  110.7 0.0 copy-done.2
  110.7 0.0 copy-done.3
  110.7 2.5 attend_head.1.att
  113.2 0.0 copy-start
  113.2 1.0 copy-done
  114.2 0.0 copy-start.4
  114.2 121.3 %return_heads.1 = bf16[256,3072]{1,0:T(8,128)(2,1)} custom-call(bf16[16,256,128]{2,1,0:T(8,128)(2,1)} %copy-done), custom_call_target="tpu_custom_call" | custom-call | bytes 80000000 | tf_op jit(solution)/shard_map/return_heads/pallas_call | solution.py:306
  238.0 1.1 dynamic-slice_reduce_fusion.3
  239.1 0.1 convert_reduce_fusion
  239.2 0.0 all-gather.2.cloned.1.call-done
  239.3 0.0 copy-done.4
  239.3 11.6 %fusion.1 = bf16[256,2560]{1,0:T(8,128)(2,1)} fusion(bf16[256,3072]{1,0:T(8,128)(2,1)} %return_heads.1, bf16[3072,2560]{1,0:T(8,128)(2,1)} %all-gather.2.cloned.1.call-done, bf16[256,2560]{1,0:T(8,128)(2,1)S(1)} %copy-done.4, f32[2560]{0:T(1024)S(1)} %get-tuple-element.7, f32[2560]{0:T(1024)S(1)} %get-tuple-element.8, f32[2560]{0:T(1024)S(1)} %get-tuple-element.6, ...), kind=kOutput, calls=%fused_computation.2 | convolution fusion | flops 4031119360 | bytes 19964672 | tf_op jit(solution)/shard_map/dot_general | solution.py:322
  (2 shorter events, 0.0 us)
Async XLA Ops:
  6.5 232.7 %all-gather.2.cloned.1.call-start = ((), (), s32[]{:S(2)}) async-start(), calls=%async_computation | async-start | bytes 16711680 | tf_op jit(solution)/shard_map/all_gather | solution.py:272
  14.5 96.2 %copy-start.1 = (s32[4,4]{1,0:T(4,128)S(1)}, s32[4,4]{1,0:T(4,128)}, u32[]{:S(2)}) copy-start(s32[4,4]{1,0:T(4,128)} %page_table.1) | copy-start | bytes 196
  14.5 96.2 %copy-start.2 = (s32[4]{0:T(128)S(1)}, s32[4]{0:T(128)}, u32[]{:S(2)}) copy-start(s32[4]{0:T(128)} %lengths.1) | copy-start | bytes 52
  14.5 96.2 %copy-start.3 = (s32[4]{0:T(128)S(1)}, s32[4]{0:T(128)}, u32[]{:S(2)}) copy-start(s32[4]{0:T(128)} %page_count.1) | copy-start | bytes 52
  113.2 1.0 copy-start
  114.2 125.1 %copy-start.4 = (bf16[256,2560]{1,0:T(8,128)(2,1)S(1)}, bf16[256,2560]{1,0:T(8,128)(2,1)}, u32[]{:S(2)}) copy-start(bf16[256,2560]{1,0:T(8,128)(2,1)} %param.17) | copy-start | bytes 3932164
Sparse Core Ops, SparseCore 0:
  9.7 202.4 all-gather.1

commit v2 on v1

--- a/solution.py
+++ b/solution.py
@@ -29,6 +29,13 @@
     return (head < heads) & (owner_of(head, heads, n) == index), head
 
 
+def inner_chips(n):
+    inner = 1
+    while (2 * inner) ** 2 <= n // 2:
+        inner *= 2
+    return inner
+
+
 def greet_seq(n, me, tensor):
     barrier = pltpu.get_barrier_semaphore()
 
@@ -41,50 +48,162 @@
     return barrier
 
 
-def scatter_heads(n, heads, q, k, v, ck, cv, out, send_sem, recv_sem):
+def scatter_heads(
+    n, heads, wide, q, k, v, ck, cv, w, out, w_out, send_sem, recv_sem, w_send, w_recv
+):
     me, tensor = lax.axis_index("seq"), lax.axis_index("tensor")
+    inner = inner_chips(n)
+    outer = n // 2 // inner
+    a, b, c = lax.div(me, 2 * inner), lax.rem(lax.div(me, 2), inner), lax.rem(me, 2)
+    w_rows = w.shape[0]
+    own = w.at[:, pl.ds(0, wide)]
     barrier = greet_seq(n, me, tensor)
     pl.semaphore_wait(barrier, n - 1)
     mine, _ = owned_by(me, heads, n)
 
+    def index(a_at, b_at, c_at):
+        return (a_at * inner + b_at) * 2 + c_at
+
+    def slot(i):
+        return w_out.at[pl.ds(pl.multiple_of(i * w_rows, w_rows), w_rows)]
+
+    def pass_block(src, i, kind, target):
+        pltpu.make_async_remote_copy(
+            src_ref=src,
+            dst_ref=slot(i),
+            send_sem=w_send.at[kind, i],
+            recv_sem=w_recv.at[i],
+            device_id=(target, tensor),
+            device_id_type=MESH,
+        ).start()
+
+    def arrived(i):
+        pltpu.make_async_copy(slot(i), slot(i), w_recv.at[i]).wait()
+
+    def along_outer(src, i, up, down):
+        if up:
+            pl.when(a + 1 < outer)(lambda: pass_block(src, i, 0, index(a + 1, b, c)))
+        if down:
+            pl.when(a > 0)(lambda: pass_block(src, i, 1, index(a - 1, b, c)))
+
+    def along_inner(src, i, up, down):
+        if up:
+            pl.when(b + 1 < inner)(lambda: pass_block(src, i, 2, index(a, b + 1, c)))
+        if down:
+            pl.when(b > 0)(lambda: pass_block(src, i, 3, index(a, b - 1, c)))
+
+    def across(src, i):
+        pass_block(src, i, 4, index(a, b, 1 - c))
+
+    along_outer(own, me, True, True)
+    along_inner(own, me, True, True)
+    across(own, me)
+    pltpu.make_async_copy(own, slot(me), w_recv.at[me]).start()
+
     def send(step, carry):
-        head = (step + me) % heads
+        head = lax.rem(step + me, heads)
         owner = owner_of(head, heads, n)
         columns = pl.ds(pl.multiple_of(head * HD, HD), HD)
 
         @pl.when(owner == me)
         def _():
-            for a, ref in enumerate((q, k, v, ck, cv)):
-                pltpu.make_async_copy(ref.at[:, columns], out.at[a, me], recv_sem.at[a]).start()
+            for i, ref in enumerate((q, k, v, ck, cv)):
+                pltpu.make_async_copy(ref.at[:, columns], out.at[i, me], recv_sem.at[i]).start()
 
         @pl.when(owner != me)
         def _():
-            for a, ref in enumerate((q, k, v, ck, cv)):
+            for i, ref in enumerate((q, k, v, ck, cv)):
                 pltpu.make_async_remote_copy(
                     src_ref=ref.at[:, columns],
-                    dst_ref=out.at[a, me],
-                    send_sem=send_sem.at[a],
-                    recv_sem=recv_sem.at[a],
+                    dst_ref=out.at[i, me],
+                    send_sem=send_sem.at[i],
+                    recv_sem=recv_sem.at[i],
                     device_id=(owner, tensor),
                     device_id_type=MESH,
                 ).start()
 
         return carry
 
-    lax.fori_loop(0, heads, send, 0)
+    stages = [heads // 2 + (heads - heads // 2) * d // (outer - 1) for d in range(outer)]
+    lax.fori_loop(0, stages[0], send, 0)
+    for d in range(1, outer):
+
+        @pl.when(a - d >= 0)
+        def _():
+            i = index(a - d, b, c)
+            arrived(i)
+            along_outer(slot(i), i, True, False)
+            along_inner(slot(i), i, True, True)
+            across(slot(i), i)
+
+        @pl.when(a + d < outer)
+        def _():
+            i = index(a + d, b, c)
+            arrived(i)
+            along_outer(slot(i), i, False, True)
+            along_inner(slot(i), i, True, True)
+            across(slot(i), i)
+
+        lax.fori_loop(stages[d - 1], stages[d], send, 0)
+
+    for e in range(1, inner):
+
+        def inner_step(step, carry):
+            a_at = lax.rem(a + step, outer)
+
+            @pl.when(b - e >= 0)
+            def _():
+                i = index(a_at, b - e, c)
+                arrived(i)
+                along_inner(slot(i), i, True, False)
+                across(slot(i), i)
+
+            @pl.when(b + e < inner)
+            def _():
+                i = index(a_at, b + e, c)
+                arrived(i)
+                along_inner(slot(i), i, False, True)
+                across(slot(i), i)
+
+            return carry
+
+        lax.fori_loop(0, outer, inner_step, 0)
+
+    def sibling_step(chip, carry):
+        arrived(chip * 2 + (1 - c))
+        return carry
+
+    lax.fori_loop(0, n // 2, sibling_step, 0)
+    arrived(me)
+
+    def sent_step(chip, carry):
+        i = chip * 2 + c
+        a_at, b_at = lax.div(chip, inner), lax.rem(chip, inner)
+
+        def sent(kind):
+            pltpu.make_async_copy(slot(i), slot(i), w_send.at[kind, i]).wait()
+
+        pl.when((b_at == b) & (a_at <= a) & (a + 1 < outer))(lambda: sent(0))
+        pl.when((b_at == b) & (a_at >= a) & (a > 0))(lambda: sent(1))
+        pl.when((b_at <= b) & (b + 1 < inner))(lambda: sent(2))
+        pl.when((b_at >= b) & (b > 0))(lambda: sent(3))
+        sent(4)
+        return carry
+
+    lax.fori_loop(0, n // 2, sent_step, 0)
 
     @pl.when(mine)
     def _():
-        for a, ref in enumerate((q, k, v, ck, cv)):
-            pltpu.make_async_copy(out.at[a], out.at[a], recv_sem.at[a]).wait()
+        for i, ref in enumerate((q, k, v, ck, cv)):
+            pltpu.make_async_copy(out.at[i], out.at[i], recv_sem.at[i]).wait()
             if heads > 1:
                 part = ref.at[:, pl.ds(0, (heads - 1) * HD)]
-                pltpu.make_async_copy(part, part, send_sem.at[a]).wait()
+                pltpu.make_async_copy(part, part, send_sem.at[i]).wait()
 
     @pl.when(jnp.logical_not(mine))
     def _():
-        for a, ref in enumerate((q, k, v, ck, cv)):
-            pltpu.make_async_copy(ref, ref, send_sem.at[a]).wait()
+        for i, ref in enumerate((q, k, v, ck, cv)):
+            pltpu.make_async_copy(ref, ref, send_sem.at[i]).wait()
 
 
 def attend_head(n, heads, rows, window, clips, slots, lengths, page_table, page_count, r, out, scores):
@@ -242,8 +361,24 @@
         pltpu.make_async_copy(part, part, send_sem.at[0]).wait()
 
 
-def clip_index(positions, clip_ends):
-    return jnp.sum((positions[:, None] >= clip_ends[None, :]).astype(jnp.int32), axis=1)
+def project_rows(
+    clips, rows, first_tiles, lengths, timestep, attention, w_first, w_rest, hidden, *refs
+):
+    gates, out = refs[:clips], refs[clips]
+    tile = pl.program_id(0)
+    position = lax.axis_index("seq") * rows + lax.broadcasted_iota(jnp.int32, out.shape, 0)
+    gate, end = None, jnp.int32(0)
+    for c in range(clips):
+        row = gates[c][pl.ds(lax.rem(timestep[c], 8), 1), :]
+        gate = jnp.broadcast_to(row, out.shape) if gate is None else jnp.where(position >= end, row, gate)
+        end = end + lengths[c]
+
+    def finish(weight):
+        projected = jnp.dot(attention[...], weight[...], preferred_element_type=jnp.float32)
+        out[...] = (hidden[...].astype(jnp.float32) + gate * projected).astype(out.dtype)
+
+    pl.when(tile < first_tiles)(lambda: finish(w_first))
+    pl.when(tile >= first_tiles)(lambda: finish(w_rest))
 
 
 def local(
@@ -265,20 +400,30 @@
     rows, tile_width = queries.shape
     heads = tile_width // HD
     clips, slots = page_table.shape
-    seq_index = lax.axis_index("seq")
     window = min(REACH + 1, n)
     pairs = (slots + 1) // 2
 
-    weight = lax.all_gather(out_weight, "seq", axis=0, tiled=True)
-
-    received = pl.pallas_call(
-        functools.partial(scatter_heads, n, heads),
-        out_shape=jax.ShapeDtypeStruct((5, n, rows, HD), jnp.bfloat16),
-        in_specs=[ANY] * 5,
-        out_specs=ANY,
-        scratch_shapes=[pltpu.SemaphoreType.DMA((5,)), pltpu.SemaphoreType.DMA((5,))],
+    width = out_weight.shape[1]
+    tile = 256 if width % 256 == 0 else 128
+    first_tiles = (7 * (width // tile) + 5) // 10
+    wide = first_tiles * tile
+
+    received, w_first = pl.pallas_call(
+        functools.partial(scatter_heads, n, heads, wide),
+        out_shape=(
+            jax.ShapeDtypeStruct((5, n, rows, HD), jnp.bfloat16),
+            jax.ShapeDtypeStruct((n * out_weight.shape[0], wide), jnp.bfloat16),
+        ),
+        in_specs=[ANY] * 6,
+        out_specs=(ANY, ANY),
+        scratch_shapes=[
+            pltpu.SemaphoreType.DMA((5,)),
+            pltpu.SemaphoreType.DMA((5,)),
+            pltpu.SemaphoreType.DMA((5, n)),
+            pltpu.SemaphoreType.DMA((n,)),
+        ],
         compiler_params=pltpu.CompilerParams(collective_id=0, has_side_effects=True),
-        cost_estimate=pl.CostEstimate(flops=0, bytes_accessed=200_000_000, transcendentals=0),
+        cost_estimate=pl.CostEstimate(flops=0, bytes_accessed=300_000_000, transcendentals=0),
         name="scatter_heads",
     )(
         queries,
@@ -286,7 +431,10 @@
         value_tiles,
         cache_keys.reshape(rows, tile_width),
         cache_values.reshape(rows, tile_width),
+        out_weight,
     )
+    rest, received = lax.optimization_barrier((out_weight[:, wide:], received))
+    w_rest = lax.all_gather(rest, "seq", axis=0, tiled=True)
 
     attended = pl.pallas_call(
         functools.partial(attend_head, n, heads, rows, window, clips, slots),
@@ -294,7 +442,7 @@
         in_specs=[SMEM] * 3 + [VMEM],
         out_specs=VMEM,
         scratch_shapes=[pltpu.VMEM((rows, (window + pairs) * rows), jnp.float32)],
-        compiler_params=pltpu.CompilerParams(vmem_limit_bytes=50 * 1024 * 1024),
+        compiler_params=pltpu.CompilerParams(vmem_limit_bytes=56 * 1024 * 1024),
         cost_estimate=pl.CostEstimate(
             flops=4 * n * rows * window * rows * HD,
             bytes_accessed=6 * n * rows * HD * 2,
@@ -319,17 +467,34 @@
         name="return_heads",
     )(attended)
 
-    projected = jnp.dot(attention, weight, preferred_element_type=jnp.float32)
-    clip_ends = jnp.cumsum(lengths, dtype=jnp.int32)
-    positions = seq_index * rows + jnp.arange(rows, dtype=jnp.int32)
-    query_clip = clip_index(positions, clip_ends)
-    gates = [
-        lax.dynamic_slice_in_dim(gate_table, timestep[c], 1, 0) for c in range(clips)
+    features = n * out_weight.shape[0]
+    gate_specs = [
+        pl.BlockSpec((8, tile), lambda j, lengths, timestep, c=c: (lax.div(timestep[c], 8), j))
+        for c in range(clips)
     ]
-    token_gate = gates[0]
-    for c in range(1, clips):
-        token_gate = jnp.where(query_clip[:, None] == c, gates[c], token_gate)
-    return (hidden.astype(jnp.float32) + token_gate * projected).astype(jnp.bfloat16)
+    return pl.pallas_call(
+        functools.partial(project_rows, clips, rows, first_tiles),
+        out_shape=jax.ShapeDtypeStruct(hidden.shape, hidden.dtype),
+        grid_spec=pltpu.PrefetchScalarGridSpec(
+            num_scalar_prefetch=2,
+            grid=(width // tile,),
+            in_specs=[
+                pl.BlockSpec((rows, features), lambda j, *_: (0, 0)),
+                pl.BlockSpec((features, tile), lambda j, *_: (0, jnp.minimum(j, first_tiles - 1))),
+                pl.BlockSpec((features, tile), lambda j, *_: (0, jnp.maximum(j - first_tiles, 0))),
+                pl.BlockSpec((rows, tile), lambda j, *_: (0, j)),
+                *gate_specs,
+            ],
+            out_specs=pl.BlockSpec((rows, tile), lambda j, *_: (0, j)),
+        ),
+        compiler_params=pltpu.CompilerParams(vmem_limit_bytes=56 * 1024 * 1024),
+        cost_estimate=pl.CostEstimate(
+            flops=2 * rows * features * width,
+            bytes_accessed=2 * features * width,
+            transcendentals=0,
+        ),
+        name="project_rows",
+    )(lengths, timestep, attention, w_first, w_rest, hidden, *([gate_table] * clips))
 
 
 def solution(mesh):

time: 258 us -> 271 us (1.050)
  Pallas kernels: 220 us -> 255 us
  matrix products: 11.6 us -> 0 us
  between operations: 20.9 us -> 13.4 us
    pallas_call x1 -> x2, Pallas kernels: 96.2 us -> 168 us  [the longest x1 153 us: local(): pl.pallas_call(functools.partial(scatter_heads, n, heads, wide), out_shap...]
    pallas_call x1, Pallas kernels: 121 us -> 84.2 us  [local(): pl.pallas_call(functools.partial(return_heads, n, tensors, heads), out_sh...]
    dot_general x1 -> x0, matrix products: 11.6 us -> none  [local(): projected = jnp.dot(attention, weight, preferred_element_type=jnp.float32)]
  transfers between devices with their start and end apart: 1 -> 1, of which waited for: 0 -> 0; matrix products, arithmetic and copies ran while one was open for 1% -> 0% of each run, Pallas kernels for 85% -> 32%
where the time goes in v2:
time: 271 us; the launch traced here: 270 us
  Pallas kernels  255 us (94%)
  between operations  13.4 us (5%)
    pallas_call x1, Pallas kernels, local(): pl.pallas_call(functools.partial(scatter_heads, n, heads, wide), out_shap...  153 us
    pallas_call x1, Pallas kernels, local(): pl.pallas_call(functools.partial(return_heads, n, tensors, heads), out_sh...  84.2 us
    pallas_call x1, Pallas kernels, local(): pl.pallas_call(functools.partial(project_rows, clips, rows, first_tiles),...  14.2 us
  transfers between devices with their start and end apart: 1, of which 0 were waited for; matrix products, arithmetic and copies ran while one was open for 0% of the time, Pallas kernels for 32%

profile of v2, /device:TPU:29, one launch (start us, length us, event | category | flops | bytes accessed | tf_op | source)
XLA Modules:
  0.0 270.5 jit_solution(14184716644834672450)
XLA Ops:
  6.5 0.0 all-gather.2.cloned.1.call-start
  6.5 1.7 slice.3
  8.2 153.5 %scatter_heads.1 = (bf16[5,16,256,128]{3,2,1,0:T(8,128)(2,1)}, bf16[3072,1792]{1,0:T(8,128)(2,1)}) custom-call(bf16[256,1536]{1,0:T(8,128)(2,1)} %q.1, bf16[256,1536]{1,0:T(8,128)(2,1)} %k.1, bf16[256,1536]{1,0:T(8,128)(2,1)} %v.1, bf16[256,1536]{1,0:T(8,128)(2,1)} %bitcast.2, bf16[256,1536]{1,0:T(8,128)(2,1)} %bitcast.3, bf16[192,2560]{1,0:T(8,128)(2,1)} %w.1), custom_call_target="tpu_custom_call" | custom-call | bytes 300000000 | tf_op jit(solution)/shard_map/scatter_heads/pallas_call | solution.py:411
  161.7 0.0 all-gather.2.cloned.1.call-update
  161.8 3.5 %attend_head.1.att = bf16[16,256,128]{2,1,0:T(8,128)(2,1)} custom-call(s32[4]{0:T(128)} %lengths.3, s32[4,4]{1,0:T(4,128)} %page_table.1, s32[4]{0:T(128)} %page_count.1, bf16[5,16,256,128]{3,2,1,0:T(8,128)(2,1)} %get-tuple-element.10.r), custom_call_target="tpu_custom_call" | custom-call | flops 3758096384 | bytes 6291456 | tf_op jit(solution)/shard_map/attend_head/pallas_call | solution.py:439
  165.2 84.2 %return_heads.1.attention = bf16[256,3072]{1,0:T(8,128)(2,1)} custom-call(bf16[16,256,128]{2,1,0:T(8,128)(2,1)} %attend_head.1.att), custom_call_target="tpu_custom_call" | custom-call | bytes 80000000 | tf_op jit(solution)/shard_map/return_heads/pallas_call | solution.py:454
  249.4 0.0 all-gather.2.cloned.1.call-done.w_rest
  249.5 14.2 %project_rows.1 = bf16[256,2560]{1,0:T(8,128)(2,1)} custom-call(s32[4]{0:T(128)} %lengths.3, s32[4]{0:T(128)} %timestep.1, bf16[256,3072]{1,0:T(8,128)(2,1)} %return_heads.1.attention, bf16[3072,1792]{1,0:T(8,128)(2,1)} %get-tuple-element.11.w_first, bf16[3072,768]{1,0:T(8,128)(2,1)} %all-gather.2.cloned.1.call-done.w_rest, bf16[256,2560]{1,0:T(8,128)(2,1)} %hidden.1, ...), custom_call_target="tpu_custom_call" | custom-call | flops 4026531840 | bytes 15728640 | tf_op jit(solution)/shard_map/project_rows/pallas_call | solution.py:475
Async XLA Ops:
  6.5 242.9 %all-gather.2.cloned.1.call-start = ((), (), s32[]{:S(2)}) async-start(), calls=%async_computation | async-start | bytes 5013504 | tf_op jit(solution)/shard_map/all_gather | solution.py:437
Sparse Core Ops, SparseCore 0:
  161.9 62.5 all-gather.1

commit v3 on v2

--- a/solution.py
+++ b/solution.py
@@ -12,6 +12,7 @@
 PAGE = 128
 POOL = 2
 REACH = 6
+CHUNKS = 3
 
 MESH = pl.DeviceIdType.MESH
 ANY = pl.BlockSpec(memory_space=pl.ANY)
@@ -21,12 +22,17 @@
 
 
 def owner_of(head, heads, n):
-    return lax.div(head * n, heads)
+    low = lax.div(head * n, heads)
+    odd = lax.rem(lax.div(low, 2 * inner_chips(n)), 2)
+    return lax.div(head * n + odd * (heads - 1), heads)
 
 
 def owned_by(index, heads, n):
-    head = lax.div(index * heads + n - 1, n)
-    return (head < heads) & (owner_of(head, heads, n) == index), head
+    low = lax.div(index * heads, n)
+    high = lax.div(index * heads + n - 1, n)
+    is_low = owner_of(low, heads, n) == index
+    is_high = (high < heads) & (owner_of(high, heads, n) == index)
+    return is_low | is_high, jnp.where(is_low, low, high)
 
 
 def inner_chips(n):
@@ -55,14 +61,16 @@
     inner = inner_chips(n)
     outer = n // 2 // inner
     a, b, c = lax.div(me, 2 * inner), lax.rem(lax.div(me, 2), inner), lax.rem(me, 2)
-    w_rows = w.shape[0]
-    own = w.at[:, pl.ds(0, wide)]
+    w_rows = w.shape[0] // CHUNKS
     barrier = greet_seq(n, me, tensor)
     pl.semaphore_wait(barrier, n - 1)
     mine, _ = owned_by(me, heads, n)
 
     def index(a_at, b_at, c_at):
         return (a_at * inner + b_at) * 2 + c_at
+
+    def own(t):
+        return w.at[pl.ds(t * w_rows, w_rows), pl.ds(0, wide)]
 
     def slot(i):
         return w_out.at[pl.ds(pl.multiple_of(i * w_rows, w_rows), w_rows)]
@@ -95,10 +103,14 @@
     def across(src, i):
         pass_block(src, i, 4, index(a, b, 1 - c))
 
-    along_outer(own, me, True, True)
-    along_inner(own, me, True, True)
-    across(own, me)
-    pltpu.make_async_copy(own, slot(me), w_recv.at[me]).start()
+    for t in range(CHUNKS):
+        along_outer(own(t), me * CHUNKS + t, True, True)
+        along_inner(own(t), me * CHUNKS + t, True, True)
+    for t in range(CHUNKS):
+        across(own(t), me * CHUNKS + t)
+        pltpu.make_async_copy(
+            own(t), slot(me * CHUNKS + t), w_recv.at[me * CHUNKS + t]
+        ).start()
 
     def send(step, carry):
         head = lax.rem(step + me, heads)
@@ -124,60 +136,67 @@
 
         return carry
 
-    stages = [heads // 2 + (heads - heads // 2) * d // (outer - 1) for d in range(outer)]
+    stages = [heads * (d + 1) // outer for d in range(outer)]
     lax.fori_loop(0, stages[0], send, 0)
     for d in range(1, outer):
 
-        @pl.when(a - d >= 0)
-        def _():
-            i = index(a - d, b, c)
-            arrived(i)
-            along_outer(slot(i), i, True, False)
-            along_inner(slot(i), i, True, True)
-            across(slot(i), i)
-
-        @pl.when(a + d < outer)
-        def _():
-            i = index(a + d, b, c)
-            arrived(i)
-            along_outer(slot(i), i, False, True)
-            along_inner(slot(i), i, True, True)
-            across(slot(i), i)
-
+        def outer_step(t, carry):
+            @pl.when(a - d >= 0)
+            def _():
+                i = index(a - d, b, c) * CHUNKS + t
+                arrived(i)
+                along_outer(slot(i), i, True, False)
+                along_inner(slot(i), i, True, True)
+                across(slot(i), i)
+
+            @pl.when(a + d < outer)
+            def _():
+                i = index(a + d, b, c) * CHUNKS + t
+                arrived(i)
+                along_outer(slot(i), i, False, True)
+                along_inner(slot(i), i, True, True)
+                across(slot(i), i)
+
+            return carry
+
+        lax.fori_loop(0, CHUNKS, outer_step, 0)
         lax.fori_loop(stages[d - 1], stages[d], send, 0)
 
     for e in range(1, inner):
 
         def inner_step(step, carry):
-            a_at = lax.rem(a + step, outer)
+            a_at, t = lax.rem(a + lax.div(step, CHUNKS), outer), lax.rem(step, CHUNKS)
 
             @pl.when(b - e >= 0)
             def _():
-                i = index(a_at, b - e, c)
+                i = index(a_at, b - e, c) * CHUNKS + t
                 arrived(i)
                 along_inner(slot(i), i, True, False)
                 across(slot(i), i)
 
             @pl.when(b + e < inner)
             def _():
-                i = index(a_at, b + e, c)
+                i = index(a_at, b + e, c) * CHUNKS + t
                 arrived(i)
                 along_inner(slot(i), i, False, True)
                 across(slot(i), i)
 
             return carry
 
-        lax.fori_loop(0, outer, inner_step, 0)
-
-    def sibling_step(chip, carry):
-        arrived(chip * 2 + (1 - c))
+        lax.fori_loop(0, outer * CHUNKS, inner_step, 0)
+
+    def sibling_step(step, carry):
+        chip, t = lax.div(step, CHUNKS), lax.rem(step, CHUNKS)
+        arrived((chip * 2 + (1 - c)) * CHUNKS + t)
         return carry
 
-    lax.fori_loop(0, n // 2, sibling_step, 0)
-    arrived(me)
-
-    def sent_step(chip, carry):
-        i = chip * 2 + c
+    lax.fori_loop(0, n // 2 * CHUNKS, sibling_step, 0)
+    for t in range(CHUNKS):
+        arrived(me * CHUNKS + t)
+
+    def sent_step(step, carry):
+        chip, t = lax.div(step, CHUNKS), lax.rem(step, CHUNKS)
+        i = (chip * 2 + c) * CHUNKS + t
         a_at, b_at = lax.div(chip, inner), lax.rem(chip, inner)
 
         def sent(kind):
@@ -190,7 +209,7 @@
         sent(4)
         return carry
 
-    lax.fori_loop(0, n // 2, sent_step, 0)
+    lax.fori_loop(0, n // 2 * CHUNKS, sent_step, 0)
 
     @pl.when(mine)
     def _():
@@ -267,9 +286,6 @@
             last = (end - 1) // rows
             span = last - first + 1
             count = page_count[c]
-            pairs = (slots + 1) // 2
-            small = min((window + 1) // 2, window)
-
             def run(token_blocks, page_pairs):
                 base = jnp.minimum(first, n - token_blocks)
 
@@ -279,8 +295,11 @@
 
                 lax.fori_loop(first, last + 1, step, 0)
 
-            for token_blocks, fits in ((small, span <= small), (window, span > small)):
-                for page_pairs, named in ((0, count <= 0), (pairs, count > 0)):
+            sizes = [size for size in (3, 5, 6) if size < window] + [window]
+            for below, token_blocks in zip([0] + sizes, sizes):
+                fits = (span > below) & (span <= token_blocks)
+                for page_pairs in range((slots + 1) // 2 + 1):
+                    named = (count > 2 * page_pairs - 2) & (count <= 2 * page_pairs)
                     pl.when(fits & named)(functools.partial(run, token_blocks, page_pairs))
             return end
 
@@ -404,8 +423,8 @@
     pairs = (slots + 1) // 2
 
     width = out_weight.shape[1]
-    tile = 256 if width % 256 == 0 else 128
-    first_tiles = (7 * (width // tile) + 5) // 10
+    tile = width // 5
+    first_tiles = 4
     wide = first_tiles * tile
 
     received, w_first = pl.pallas_call(
@@ -419,8 +438,8 @@
         scratch_shapes=[
             pltpu.SemaphoreType.DMA((5,)),
             pltpu.SemaphoreType.DMA((5,)),
-            pltpu.SemaphoreType.DMA((5, n)),
-            pltpu.SemaphoreType.DMA((n,)),
+            pltpu.SemaphoreType.DMA((5, n * CHUNKS)),
+            pltpu.SemaphoreType.DMA((n * CHUNKS,)),
         ],
         compiler_params=pltpu.CompilerParams(collective_id=0, has_side_effects=True),
         cost_estimate=pl.CostEstimate(flops=0, bytes_accessed=300_000_000, transcendentals=0),

time: 271 us -> 250 us (0.923)
  Pallas kernels: 255 us -> 235 us
    pallas_call x1, Pallas kernels: 84.2 us -> 52.7 us  [local(): pl.pallas_call(functools.partial(return_heads, n, tensors, heads), out_sh...]
    pallas_call x1, Pallas kernels: 3.49 us -> 25.3 us  [local(): pl.pallas_call(functools.partial(attend_head, n, heads, rows, window, cli...]
    pallas_call x1, Pallas kernels: 153 us -> 146 us  [local(): pl.pallas_call(functools.partial(scatter_heads, n, heads, wide), out_shap...]
  transfers between devices with their start and end apart: 1 -> 1, of which waited for: 0 -> 0; matrix products, arithmetic and copies ran while one was open for 0% -> 0% of each run, Pallas kernels for 32% -> 31%
where the time goes in v3:
time: 250 us
  Pallas kernels  235 us (94%)
  between operations  13.4 us (5%)
    pallas_call x1, Pallas kernels, local(): pl.pallas_call(functools.partial(scatter_heads, n, heads, wide), out_shap...  146 us
    pallas_call x1, Pallas kernels, local(): pl.pallas_call(functools.partial(return_heads, n, tensors, heads), out_sh...  52.7 us
    pallas_call x1, Pallas kernels, local(): pl.pallas_call(functools.partial(attend_head, n, heads, rows, window, cli...  25.3 us
    pallas_call x1, Pallas kernels, local(): pl.pallas_call(functools.partial(project_rows, clips, rows, first_tiles),...  11.8 us
  transfers between devices with their start and end apart: 1, of which 0 were waited for; matrix products, arithmetic and copies ran while one was open for 0% of the time, Pallas kernels for 31%

profile of v3, /device:TPU:29, one launch (start us, length us, event | category | flops | bytes accessed | tf_op | source)
XLA Modules:
  0.0 250.4 jit_solution(5717132515721349517)
XLA Ops:
  6.5 0.0 all-gather.2.cloned.1.call-start
  6.5 1.6 slice.3
  8.1 145.6 %scatter_heads.1 = (bf16[5,16,256,128]{3,2,1,0:T(8,128)(2,1)}, bf16[3072,2048]{1,0:T(8,128)(2,1)}) custom-call(bf16[256,1536]{1,0:T(8,128)(2,1)} %q.1, bf16[256,1536]{1,0:T(8,128)(2,1)} %k.1, bf16[256,1536]{1,0:T(8,128)(2,1)} %v.1, bf16[256,1536]{1,0:T(8,128)(2,1)} %bitcast.2, bf16[256,1536]{1,0:T(8,128)(2,1)} %bitcast.3, bf16[192,2560]{1,0:T(8,128)(2,1)} %w.1), custom_call_target="tpu_custom_call" | custom-call | bytes 300000000 | tf_op jit(solution)/shard_map/scatter_heads/pallas_call | solution.py:430
  153.7 0.0 all-gather.2.cloned.1.call-update
  153.8 25.3 %attend_head.1.att = bf16[16,256,128]{2,1,0:T(8,128)(2,1)} custom-call(s32[4]{0:T(128)} %lengths.3, s32[4,4]{1,0:T(4,128)} %page_table.1, s32[4]{0:T(128)} %page_count.1, bf16[5,16,256,128]{3,2,1,0:T(8,128)(2,1)} %get-tuple-element.10.r), custom_call_target="tpu_custom_call" | custom-call | flops 3758096384 | bytes 6291456 | tf_op jit(solution)/shard_map/attend_head/pallas_call | solution.py:458
  179.1 52.7 %return_heads.1.attention = bf16[256,3072]{1,0:T(8,128)(2,1)} custom-call(bf16[16,256,128]{2,1,0:T(8,128)(2,1)} %attend_head.1.att), custom_call_target="tpu_custom_call" | custom-call | bytes 80000000 | tf_op jit(solution)/shard_map/return_heads/pallas_call | solution.py:473
  231.8 0.0 all-gather.2.cloned.1.call-done.w_rest
  231.8 11.8 %project_rows.1 = bf16[256,2560]{1,0:T(8,128)(2,1)} custom-call(s32[4]{0:T(128)} %lengths.3, s32[4]{0:T(128)} %timestep.1, bf16[256,3072]{1,0:T(8,128)(2,1)} %return_heads.1.attention, bf16[3072,2048]{1,0:T(8,128)(2,1)} %get-tuple-element.11.w_first, bf16[3072,512]{1,0:T(8,128)(2,1)} %all-gather.2.cloned.1.call-done.w_rest, bf16[256,2560]{1,0:T(8,128)(2,1)} %hidden.1, ...), custom_call_target="tpu_custom_call" | custom-call | flops 4026531840 | bytes 15728640 | tf_op jit(solution)/shard_map/project_rows/pallas_call | solution.py:494
Async XLA Ops:
  6.5 225.2 %all-gather.2.cloned.1.call-start = ((), (), s32[]{:S(2)}) async-start(), calls=%async_computation | async-start | bytes 3342336 | tf_op jit(solution)/shard_map/all_gather | solution.py:456
Sparse Core Ops, SparseCore 0:
  153.9 54.6 all-gather.1

commit v4 on v3

--- a/solution.py
+++ b/solution.py
@@ -424,8 +424,10 @@
 
     width = out_weight.shape[1]
     tile = width // 5
-    first_tiles = 4
+    first_tiles = 3
     wide = first_tiles * tile
+
+    w_rest = lax.all_gather(out_weight[:, wide:], "seq", axis=0, tiled=True)
 
     received, w_first = pl.pallas_call(
         functools.partial(scatter_heads, n, heads, wide),
@@ -452,9 +454,6 @@
         cache_values.reshape(rows, tile_width),
         out_weight,
     )
-    rest, received = lax.optimization_barrier((out_weight[:, wide:], received))
-    w_rest = lax.all_gather(rest, "seq", axis=0, tiled=True)
-
     attended = pl.pallas_call(
         functools.partial(attend_head, n, heads, rows, window, clips, slots),
         out_shape=jax.ShapeDtypeStruct((n, rows, HD), jnp.bfloat16),

time: 250 us -> 258 us (1.032)
  Pallas kernels: 235 us -> 243 us
    pallas_call x1, Pallas kernels: 146 us -> 159 us  [local(): pl.pallas_call(functools.partial(scatter_heads, n, heads, wide), out_shap...]
    pallas_call x1, Pallas kernels: 52.7 us -> 48.6 us  [local(): pl.pallas_call(functools.partial(return_heads, n, tensors, heads), out_sh...]
  transfers between devices with their start and end apart: 1 -> 1, of which waited for: 0 -> 0; matrix products, arithmetic and copies ran while one was open for 0% -> 0% of each run, Pallas kernels for 31% -> 89%
where the time goes in v4:
time: 258 us; the launch traced here: 259 us
  Pallas kernels  243 us (94%)
  between operations  13.4 us (5%)
    pallas_call x1, Pallas kernels, local(): pl.pallas_call(functools.partial(scatter_heads, n, heads, wide), out_shap...  159 us
    pallas_call x1, Pallas kernels, local(): pl.pallas_call(functools.partial(return_heads, n, tensors, heads), out_sh...  48.6 us
    pallas_call x1, Pallas kernels, local(): pl.pallas_call(functools.partial(attend_head, n, heads, rows, window, cli...  23.4 us
    pallas_call x1, Pallas kernels, local(): pl.pallas_call(functools.partial(project_rows, clips, rows, first_tiles),...  12.3 us
  transfers between devices with their start and end apart: 1, of which 0 were waited for; matrix products, arithmetic and copies ran while one was open for 0% of the time, Pallas kernels for 89%

profile of v4, /device:TPU:29, one launch (start us, length us, event | category | flops | bytes accessed | tf_op | source)
XLA Modules:
  0.0 258.6 jit_solution(295588076307988140)
XLA Ops:
  6.5 0.0 all-gather.2.cloned.1.call-start
  6.5 1.8 slice.3
  8.3 0.0 all-gather.2.cloned.1.call-update
  8.3 159.1 %scatter_heads.1 = (bf16[5,16,256,128]{3,2,1,0:T(8,128)(2,1)}, bf16[3072,1536]{1,0:T(8,128)(2,1)}) custom-call(bf16[256,1536]{1,0:T(8,128)(2,1)} %q.1, bf16[256,1536]{1,0:T(8,128)(2,1)} %k.1, bf16[256,1536]{1,0:T(8,128)(2,1)} %v.1, bf16[256,1536]{1,0:T(8,128)(2,1)} %bitcast.2, bf16[256,1536]{1,0:T(8,128)(2,1)} %bitcast.3, bf16[192,2560]{1,0:T(8,128)(2,1)} %w.1), custom_call_target="tpu_custom_call" | custom-call | bytes 300000000 | tf_op jit(solution)/shard_map/scatter_heads/pallas_call | solution.py:432
  167.5 23.4 %attend_head.1.att = bf16[16,256,128]{2,1,0:T(8,128)(2,1)} custom-call(s32[4]{0:T(128)} %lengths.3, s32[4,4]{1,0:T(4,128)} %page_table.1, s32[4]{0:T(128)} %page_count.1, bf16[5,16,256,128]{3,2,1,0:T(8,128)(2,1)} %get-tuple-element.7.r), custom_call_target="tpu_custom_call" | custom-call | flops 3758096384 | bytes 6291456 | tf_op jit(solution)/shard_map/attend_head/pallas_call | solution.py:457
  190.9 48.6 %return_heads.1.attention = bf16[256,3072]{1,0:T(8,128)(2,1)} custom-call(bf16[16,256,128]{2,1,0:T(8,128)(2,1)} %attend_head.1.att), custom_call_target="tpu_custom_call" | custom-call | bytes 80000000 | tf_op jit(solution)/shard_map/return_heads/pallas_call | solution.py:472
  239.5 0.0 all-gather.2.cloned.1.call-done.w_rest
  239.5 12.3 %project_rows.1 = bf16[256,2560]{1,0:T(8,128)(2,1)} custom-call(s32[4]{0:T(128)} %lengths.3, s32[4]{0:T(128)} %timestep.1, bf16[256,3072]{1,0:T(8,128)(2,1)} %return_heads.1.attention, bf16[3072,1536]{1,0:T(8,128)(2,1)} %get-tuple-element.8.w_first, bf16[3072,1024]{1,0:T(8,128)(2,1)} %all-gather.2.cloned.1.call-done.w_rest, bf16[256,2560]{1,0:T(8,128)(2,1)} %hidden.1, ...), custom_call_target="tpu_custom_call" | custom-call | flops 4026531840 | bytes 15728640 | tf_op jit(solution)/shard_map/project_rows/pallas_call | solution.py:493
Async XLA Ops:
  6.5 233.0 %all-gather.2.cloned.1.call-start = ((), (), s32[]{:S(2)}) async-start(), calls=%async_computation | async-start | bytes 6684672 | tf_op jit(solution)/shard_map/all_gather | solution.py:430
Sparse Core Ops, SparseCore 0:
  9.6 154.2 all-gather.1
